TPU v7x, 512 devices: a whole 4x4x16 slice. The times are simulated.
512 devices in a mesh: resp: 16 (over x_lo, y, core), ctx: 32 (over z, x_hi).
Axes of the slice: x: 4 (x_hi: 2, x_lo: 2; x = x_hi * 2 + x_lo), y: 4, z: 16, core: 2. Of those that a mesh axis runs over, the one named last changes fastest.
Arguments:
- queries: bfloat16 [32, 2048, 8, 128], P('resp', 'ctx'), may hold values from -170 to 170
- prompt_keys: bfloat16 [512, 128], P('ctx'), may hold values from -6 to 6
- prompt_values: bfloat16 [512, 128], P('ctx'), may hold values from -6 to 6
- resp_keys: bfloat16 [32, 2048, 128], P('resp', 'ctx'), may hold values from -6 to 6
- resp_values: bfloat16 [32, 2048, 128], P('resp', 'ctx'), may hold values from -6 to 6
- upstream: bfloat16 [32, 2048, 8, 128], P('resp', 'ctx'), may hold values from -6 to 6
- behav_logp: float32 [32, 2048], P('resp', 'ctx'), may hold values from -2.5 to -0.1
- cur_logp: float32 [32, 2048], P('resp', 'ctx'), may hold values from -2.5 to -0.1
- advantages: float32 [32], P('resp'), may hold values from -4 to 4
- lengths: int32 [32], P('resp'), may hold values from 128 to 2048, as said below
Outputs:
- grad_queries: bfloat16 [32, 2048, 8, 128], P('resp', 'ctx')
- grad_resp_keys: bfloat16 [32, 2048, 128], P('resp', 'ctx')
- grad_resp_values: bfloat16 [32, 2048, 128], P('resp', 'ctx')
- grad_prompt_keys: float32 [512, 128], P('ctx')
- grad_prompt_values: float32 [512, 128], P('ctx')
Inputs may be any that keep to these rules, and one draw needn't show every extreme that they name: `lengths`: each length is a multiple of 128; in every draw one response has length 2048 and another has length 128.
All inputs are finite; a program needn't handle non-finite values.
Results may differ from a plain program's by a relative error of at most 0.024.
Values may be sent and summed in bfloat16 or wider, within the bound.
A program may use at most 64 MiB of HBM per device.

v0:
```python
import jax
import jax.numpy as jnp
from jax import lax
from jax.sharding import PartitionSpec as P

RATIO_CAP = 2.0


def token_weights(advantages, behav_logp, cur_logp, lengths, positions, full_len):
    ratio = jnp.minimum(jnp.exp(cur_logp - behav_logp), RATIO_CAP)
    valid = (positions[None, :] < lengths[:, None]).astype(jnp.float32)
    spread = full_len / lengths.astype(jnp.float32)
    return -advantages[:, None] * ratio * valid * spread[:, None]


def attend_block(query_rows, grad_rows, keys_all, values_all, row_pos, col_pos, softmax_scale):
    scores = jnp.dot(query_rows, keys_all.T, preferred_element_type=jnp.float32) * softmax_scale
    scores = jnp.where(col_pos[None, :] <= row_pos[:, None], scores, -jnp.inf)
    row_max = jnp.max(scores, axis=1, keepdims=True)
    shifted = jnp.exp(scores - row_max)
    probs = lax.optimization_barrier(
        (shifted / jnp.sum(shifted, axis=1, keepdims=True)).astype(jnp.bfloat16)
    )
    attended = lax.optimization_barrier(
        jnp.dot(probs, values_all, preferred_element_type=jnp.float32).astype(jnp.bfloat16)
    )
    deltas = jnp.sum(grad_rows.astype(jnp.float32) * attended.astype(jnp.float32), axis=1)
    grad_probs = jnp.dot(grad_rows, values_all.T, preferred_element_type=jnp.float32)
    grad_scores = (probs.astype(jnp.float32) * (grad_probs - deltas[:, None])).astype(jnp.bfloat16)
    query_grad = (
        jnp.dot(grad_scores, keys_all, preferred_element_type=jnp.float32) * softmax_scale
    ).astype(jnp.bfloat16)
    return (probs, grad_scores, query_grad)


def per_device(
    queries,
    prompt_keys,
    prompt_values,
    resp_keys,
    resp_values,
    upstream,
    behav_logp,
    cur_logp,
    advantages,
    lengths,
):
    resp_dev, tok_dev, heads, head_dim = queries.shape
    softmax_scale = head_dim ** (-0.5)
    ctx_size = lax.axis_size("ctx")
    full_len = tok_dev * ctx_size
    local_prompt = prompt_keys.shape[0]
    all_prompt_keys, all_prompt_values, all_resp_keys, all_resp_values = (
        lax.all_gather(prompt_keys, "ctx", axis=0, tiled=True),
        lax.all_gather(prompt_values, "ctx", axis=0, tiled=True),
        lax.all_gather(resp_keys, "ctx", axis=1, tiled=True),
        lax.all_gather(resp_values, "ctx", axis=1, tiled=True),
    )
    prompt_len = all_prompt_keys.shape[0]
    positions = lax.axis_index("ctx") * tok_dev + jnp.arange(tok_dev, dtype=jnp.int32)
    weights = token_weights(advantages, behav_logp, cur_logp, lengths, positions, full_len)
    grad_out = (weights[:, :, None, None] * upstream.astype(jnp.float32)).astype(jnp.bfloat16)
    row_pos = jnp.repeat(positions, heads)
    col_pos = jnp.concatenate(
        [jnp.full((prompt_len,), -1, jnp.int32), jnp.arange(full_len, dtype=jnp.int32)]
    )
    query_rows = queries.reshape(resp_dev, tok_dev * heads, head_dim)
    grad_rows = grad_out.reshape(resp_dev, tok_dev * heads, head_dim)
    prob_list = []
    score_list = []
    query_list = []
    for member in range(resp_dev):
        keys_all = jnp.concatenate([all_prompt_keys, all_resp_keys[member]], 0)
        values_all = jnp.concatenate([all_prompt_values, all_resp_values[member]], 0)
        probs, grad_scores, query_grad = attend_block(
            query_rows[member],
            grad_rows[member],
            keys_all,
            values_all,
            row_pos,
            col_pos,
            softmax_scale,
        )
        prob_list.append(probs)
        score_list.append(grad_scores)
        query_list.append(query_grad)
    grad_queries = jnp.stack(query_list).reshape(queries.shape)

    def member_term(member, row_count, offset):
        score_cols = lax.dynamic_slice_in_dim(score_list[member], offset, row_count, 1)
        prob_cols = lax.dynamic_slice_in_dim(prob_list[member], offset, row_count, 1)
        key_part = (
            jnp.dot(score_cols.T, query_rows[member], preferred_element_type=jnp.float32)
            * softmax_scale
        )
        value_part = jnp.dot(prob_cols.T, grad_rows[member], preferred_element_type=jnp.float32)
        return jnp.concatenate([key_part, value_part], 1)

    row_count = tok_dev * lax.axis_size("ctx")
    part_list = []
    for member in range(resp_dev):
        part_list.append(member_term(member, row_count, prompt_len))
    response_sums = lax.psum_scatter(
        jnp.stack(part_list, 1).astype(jnp.bfloat16), "ctx", scatter_dimension=0, tiled=True
    ).astype(jnp.float32)
    response_grads = jnp.transpose(response_sums, (1, 0, 2)).astype(jnp.bfloat16)
    summed = member_term(0, local_prompt * lax.axis_size("ctx"), 0)
    member = 1
    summed = summed + member_term(member, local_prompt * lax.axis_size("ctx"), 0)
    ctx_share = lax.psum_scatter(
        summed.astype(jnp.bfloat16), "ctx", scatter_dimension=0, tiled=True
    ).astype(jnp.float32)
    prompt_total = lax.psum(ctx_share, "resp")
    return (
        grad_queries,
        response_grads[:, :, :head_dim],
        response_grads[:, :, head_dim:],
        prompt_total[:, :head_dim],
        prompt_total[:, head_dim:],
    )


def solution(mesh):
    placed = (
        P("resp", "ctx", None, None),
        P("ctx", None),
        P("ctx", None),
        P("resp", "ctx", None),
        P("resp", "ctx", None),
        P("resp", "ctx", None, None),
        P("resp", "ctx"),
        P("resp", "ctx"),
        P("resp"),
        P("resp"),
    )
    return jax.shard_map(
        per_device,
        mesh=mesh,
        in_specs=placed,
        out_specs=(
            P("resp", "ctx", None, None),
            P("resp", "ctx", None),
            P("resp", "ctx", None),
            P("ctx", None),
            P("ctx", None),
        ),
        check_vma=False,
    )
```

profile of v0, /device:TPU:1, one launch (start us, length us, event | category | flops | bytes accessed | tf_op | source)
XLA Modules:
  0.0 1248.4 jit_solution(14666977171961471624)
XLA Ops:
  7.2 0.0 copy-start.12
  7.2 0.0 copy-start.10
  7.2 0.0 all-gather.3.cloned.1.call-start
  7.2 0.7 all-gather.3.cloned.1.call-update
  7.9 0.0 all-gather.5.cloned.1.call-start
  8.0 0.7 all-gather.5.cloned.1.call-update
  8.7 0.0 reduce-scatter.2.cloned.1.call-start
  8.7 69.9 %all_gather.12 = bf16[512,128]{1,0:T(8,128)(2,1)S(1)} all-gather(bf16[16,128]{1,0:T(8,128)(2,1)} %param.11), channel_id=1, replica_groups=mesh['resp'=16,'ctx'=32] {'ctx'}, dimensions={0}, use_global_device_ids=true | all-gather | bytes 135168 | tf_op jit(solution)/shard_map/all_gather | solution.py:54
  78.7 0.1 broadcast_in_dim.6
  78.7 0.1 le.9
  78.8 57.9 %all_gather.14 = bf16[512,128]{1,0:T(8,128)(2,1)S(1)} all-gather(bf16[16,128]{1,0:T(8,128)(2,1)} %param.12), channel_id=1, replica_groups=mesh['resp'=16,'ctx'=32] {'ctx'}, dimensions={0}, use_global_device_ids=true | all-gather | bytes 135168 | tf_op jit(solution)/shard_map/all_gather | solution.py:55
  136.8 0.7 convert_divide_fusion
  137.4 0.7 neg.4
  138.1 0.8 fusion.31
  138.8 1.2 multiply_convert_fusion.2
  140.0 10.4 all-gather.3.cloned.1.call-done
  150.4 1.3 slice_bitcast_fusion.3
  151.7 0.0 copy-start.3
  151.7 0.0 copy-done.12
  151.7 0.0 copy-done.10
  151.7 0.9 fusion.43
  152.6 0.0 copy-done.7
  152.6 0.0 copy-done.3
  152.6 0.8 fusion
  153.4 0.9 divide_convert_fusion.1
  154.3 136.6 %all-gather.5.cloned.1.call-done = bf16[2,2048,128]{2,1,0:T(8,128)(2,1)} async-done(((bf16[2,64,128]{2,1,0:T(8,128)(2,1)}), bf16[2,2048,128]{2,1,0:T(8,128)(2,1)}) %all-gather.5.cloned.1.call-update) | async-done | bytes 1048592 | tf_op jit(solution)/shard_map/all_gather | solution.py:57
  290.9 1.3 slice_bitcast_fusion
  292.2 0.9 convolution_convert_fusion.3
  293.1 0.0 copy-done.8
  293.1 0.0 copy-done.11
  293.1 0.9 fusion.42
  294.0 0.8 fusion.1
  294.8 0.9 divide_convert_fusion
  295.6 0.3 fusion.15
  295.9 0.3 fusion.12
  296.2 0.9 convolution_convert_fusion.2
  297.1 0.2 multiply_reduce_fusion.1
  297.4 0.8 multiply_convert_fusion.1
  298.2 0.3 convolution_multiply_fusion.3
  298.5 1.6 fusion.2
  300.2 0.8 multiply_convert_fusion
  301.0 0.3 convolution_multiply_fusion.2
  301.3 1.6 fusion.3
  303.0 1.6 convolution_convert_fusion.1
  304.6 0.8 convolution_convert_fusion
  305.4 0.7 fusion.18
  306.2 0.0 reduce-scatter.2.cloned.1.call-update
  306.2 0.2 all-reduce.3.cloned.1.call-start
  306.4 0.1 maximum_bitcast_fusion
  306.6 0.2 pad_maximum_fusion
  306.8 0.0 copy-start.9
  306.8 3.9 copy.33
  310.7 0.0 all-reduce.3.cloned.1.call-update
  310.8 1.4 dynamic-slice
  312.8 2.7 fusion.11
  315.6 0.9 fusion.10
  316.5 0.7 pad_maximum_fusion.13
  317.2 616.7 %reduce-scatter.2.cloned.1.call-done = bf16[16,256]{1,0:T(8,128)(2,1)} async-done(((bf16[512,256]{1,0:T(8,128)(2,1)}), bf16[16,256]{1,0:T(8,128)(2,1)}) %reduce-scatter.2.cloned.1.call-update) | async-done | bytes 8208 | tf_op jit(solution)/shard_map/reduce_scatter | solution.py:110
  933.9 61.8 %psum.7 = f32[16,256]{1,0:T(8,128)S(1)} all-reduce(bf16[16,256]{1,0:T(8,128)(2,1)} %reduce-scatter.2.cloned.1.call-done), channel_id=1, replica_groups=mesh['resp'=16,'ctx'=32] {'resp'}, use_global_device_ids=true, to_apply=%region_8.9 | all-reduce | flops 4096 | bytes 24576 | tf_op jit(solution)/shard_map/psum | solution.py:113
  995.8 0.6 fusion.41
  996.4 243.3 %all-reduce.3.cloned.1.call-done = bf16[2048,2,256]{2,1,0:T(2,128)(2,1)} async-done(((bf16[2048,2,256]{2,1,0:T(2,128)(2,1)}), bf16[2048,2,256]{2,1,0:T(2,128)(2,1)}) %all-reduce.3.cloned.1.call-update) | async-done | bytes 2097168
  1239.6 0.9 dynamic-slice_bitcast_fusion
  1240.6 0.6 copy.38
  1241.2 0.6 copy.39
  (18 shorter events, 0.1 us)
Async XLA Ops:
  7.2 144.6 %copy-start.12 = (s32[2560]{0:T(1024)S(1)}, s32[2560]{0:T(1024)}, u32[]{:S(2)}) copy-start(s32[2560]{0:T(1024)} %constant.8.clone.1) | copy-start | bytes 30724
  7.2 144.6 %copy-start.10 = (bf16[2,64,8,128]{3,2,1,0:T(8,128)(2,1)S(1)}, bf16[2,64,8,128]{3,2,1,0:T(8,128)(2,1)}, u32[]{:S(2)}) copy-start(bf16[2,64,8,128]{3,2,1,0:T(8,128)(2,1)} %param.10) | copy-start | bytes 786436
  7.2 143.2 %all-gather.3.cloned.1.call-start = ((), (), s32[]{:S(2)}) async-start(), calls=%async_computation.1 | async-start | bytes 1081344 | tf_op jit(solution)/shard_map/all_gather | solution.py:56
  7.9 283.0 %all-gather.5.cloned.1.call-start = ((), (), s32[]{:S(2)}) async-start(), calls=%async_computation.2 | async-start | bytes 1081344 | tf_op jit(solution)/shard_map/all_gather | solution.py:57
  8.7 925.2 %reduce-scatter.2.cloned.1.call-start = ((), (), s32[]{:S(2)}) async-start(), calls=%async_computation.3 | async-start | bytes 270336 | tf_op jit(solution)/shard_map/reduce_scatter | solution.py:110
  78.7 74.0 %copy-start.7 = (bf16[512,128]{1,0:T(8,128)(2,1)}, bf16[512,128]{1,0:T(8,128)(2,1)S(1)}, u32[]{:S(2)}) copy-start(bf16[512,128]{1,0:T(8,128)(2,1)S(1)} %all_gather.12) | copy-start | bytes 393220
  151.7 0.9 copy-start.3
  290.9 2.2 copy-start.8
  290.9 2.2 copy-start.11
  298.2 2.8 copy-start
  301.0 3.6 copy-start.1
  304.6 1.8 copy-start.4
  304.6 1.8 copy-start.5
  304.6 1.9 copy-start.6
  306.2 933.5 %all-reduce.3.cloned.1.call-start = ((), (), s32[]{:S(2)}) async-start(), calls=%async_computation.4 | async-start | bytes 4194304
  306.8 6.0 copy-start.9
  310.7 4.8 copy-start.2
Sparse Core Ops, SparseCore 0:
  11.1 139.2 all-gather.2
  153.6 137.2 all-gather.4
  306.3 627.5 reduce-scatter.1
  936.7 302.9 all-reduce.2
where the time goes:
time: 1270 us; the launch traced here: 1250 us
  waiting for transfers between devices  1010 us (80%)
  blocking collectives  190 us (15%)
  matrix products  15.7 us (1%)
  between operations  14.7 us (1%)
    reduce_scatter x1, waiting for transfers between devices, per_device(): lax.psum_scatter(summed.astype(jnp.bfloat16), 'ctx', scatter_dimension=0,...  617 us
    unnamed x5, waiting for transfers between devices  245 us
    all_gather x1, waiting for transfers between devices, per_device(): lax.all_gather(resp_values, 'ctx', axis=1, tiled=True)  137 us
    all_gather x1, blocking collectives, per_device(): lax.all_gather(prompt_keys, 'ctx', axis=0, tiled=True)  69.9 us
    psum x1, blocking collectives, per_device(): prompt_total = lax.psum(ctx_share, 'resp')  61.8 us
    all_gather x1, blocking collectives, per_device(): lax.all_gather(prompt_values, 'ctx', axis=0, tiled=True)  57.9 us
  transfers between devices with their start and end apart: 4, of which 4 were waited for; matrix products, arithmetic and copies ran while one was open for 1% of the time, Pallas kernels for 0%

commit v1 on v0

v1 whole, which is shorter than its diff:
```python
import functools

import jax
import jax.numpy as jnp
from jax import lax
from jax.experimental import pallas as pl
from jax.experimental.pallas import tpu as pltpu
from jax.sharding import PartitionSpec as P

RATIO_CAP = 2.0
MESH = pl.DeviceIdType.MESH
F32 = jnp.float32
BF16 = jnp.bfloat16


def kernel(
    q_ref, u_ref, pk_ref, pv_ref, rk_ref, rv_ref, behav_ref, cur_ref, adv_ref, len_ref,
    gq_ref, grk_ref, grv_ref, gpk_ref, gpv_ref,
    kv, xkv, qb, gb, gsend, qt, gt, sc, dp, mx, sm, dl, dqt, pp, part, first, rs, fin, xfin, dqs, pself, pother, pr,
    ag_s, ag_r, rs_s, rs_r, x_s, x_r, p_s, p_r,
    *, nz, nr, tok, heads, prow, full_len,
):
    hd = q_ref.shape[-1]
    scale = hd ** (-0.5)
    half = nz // 2
    rows = tok * heads
    two = 2 * rows
    key_rows = 2 * tok
    n_resp_chunks = nz
    p_chunks = (2 * nz * prow) // key_rows
    per_chunk = key_rows // (2 * prow)

    c = lax.axis_index("ctx")
    r = lax.axis_index("resp")
    z = c // 2
    h = c % 2
    g = 1 - h
    partner = {"ctx": 2 * z + g}
    up = {"ctx": 2 * ((z + 1) % nz) + h}
    down = {"ctx": 2 * ((z + nz - 1) % nz) + h}
    ring_to = (up, down)

    barrier = pltpu.get_barrier_semaphore()
    for dev in (partner, up, down):
        pl.semaphore_signal(barrier, 1, device_id=dev, device_id_type=MESH)
    for d in range(1, nr):
        pl.semaphore_signal(barrier, 1, device_id={"resp": (r + d) % nr}, device_id_type=MESH)

    k_at, v_at, pk_at, pv_at = 0, tok, 2 * tok, 2 * tok + prow
    kv[z, h, pl.ds(k_at, tok)] = rk_ref[h]
    kv[z, h, pl.ds(v_at, tok)] = rv_ref[h]
    kv[z, h, pl.ds(pk_at, prow)] = pk_ref[...]
    kv[z, h, pl.ds(pv_at, prow)] = pv_ref[...]
    xkv[pl.ds(k_at, tok)] = rk_ref[g]
    xkv[pl.ds(v_at, tok)] = rv_ref[g]
    xkv[pl.ds(pk_at, prow)] = pk_ref[...]
    xkv[pl.ds(pv_at, prow)] = pv_ref[...]

    def remote(src, dst, ssem, rsem, dev):
        return pltpu.make_async_remote_copy(
            src_ref=src, dst_ref=dst, send_sem=ssem, recv_sem=rsem, device_id=dev, device_id_type=MESH
        )

    x_kv = remote(xkv, kv.at[z, h], x_s.at[0], x_r.at[0], partner)
    x_kv_in = remote(xkv, kv.at[z, g], x_s.at[0], x_r.at[0], partner)
    x_q = remote(q_ref.at[g], qb.at[h], x_s.at[1], x_r.at[1], partner)
    x_q_in = remote(q_ref.at[g], qb.at[g], x_s.at[1], x_r.at[1], partner)
    x_g = remote(gsend, gb.at[h], x_s.at[2], x_r.at[2], partner)
    x_g_in = remote(gsend, gb.at[g], x_s.at[2], x_r.at[2], partner)

    def ag_copy(d, s, blk):
        chunk = (z - s + nz) % nz if d == 0 else (z + s) % nz
        return remote(kv.at[chunk, blk], kv.at[chunk, blk], ag_s.at[d, s, blk], ag_r.at[d, s, blk], ring_to[d])

    def ag_recv(d, s, blk):
        chunk = (z - 1 - s + 2 * nz) % nz if d == 0 else (z + 1 + s) % nz
        return remote(kv.at[chunk, blk], kv.at[chunk, blk], ag_s.at[d, s, blk], ag_r.at[d, s, blk], ring_to[d])

    pl.semaphore_wait(barrier, 2 + nr)
    x_kv.start()
    for d in range(2):
        ag_copy(d, 0, h).start()
    x_q.start()

    row_of = lax.broadcasted_iota(jnp.int32, (rows, tok), 0) // heads
    col_of = lax.broadcasted_iota(jnp.int32, (rows, tok), 1)
    position = c * tok + lax.broadcasted_iota(jnp.int32, (1, tok), 1)

    def weighted(member):
        length = jnp.full((1, tok), len_ref[member], jnp.int32)
        ratio = jnp.minimum(jnp.exp(cur_ref[pl.ds(member, 1), :] - behav_ref[pl.ds(member, 1), :]), RATIO_CAP)
        valid = (position < length).astype(F32)
        weight = -adv_ref[member] * ratio * valid * (full_len / length.astype(F32))
        spread = jnp.where(row_of == col_of, jnp.broadcast_to(weight, (rows, tok)), 0.0)
        column = jnp.sum(spread, axis=1, keepdims=True)
        return (column * u_ref[member].astype(F32)).astype(BF16)

    gsend[...] = weighted(g)
    x_g.start()
    gb[h] = weighted(h)
    qb[h] = q_ref[h]

    x_kv_in.wait_recv()
    for d in range(2):
        ag_copy(d, 0, g).start()
    x_q_in.wait_recv()
    qt[...] = qb[...].reshape(two, hd).T
    x_g_in.wait_recv()
    gt[...] = gb[...].reshape(two, hd).T

    def scores_of(keys, values):
        s = jnp.dot(keys, qt[...], preferred_element_type=F32) * scale
        return s, jnp.dot(values, gt[...], preferred_element_type=F32)

    def chunk_of(j, at):
        return kv[j, :, pl.ds(at, tok), :].reshape(key_rows, hd)

    def prompt_of(i, at):
        return kv[pl.ds(i * per_chunk, per_chunk), :, pl.ds(at, prow), :].reshape(key_rows, hd)

    s, grad_p = scores_of(chunk_of(z, k_at), chunk_of(z, v_at))
    key_pos = lax.broadcasted_iota(jnp.int32, (key_rows, two), 0)
    row_pos = lax.broadcasted_iota(jnp.int32, (key_rows, two), 1) // heads
    s = jnp.where(key_pos <= row_pos, s, -jnp.inf)
    sc[z] = s
    dp[z] = grad_p
    m = jnp.max(s, axis=0, keepdims=True)
    e = jnp.exp(s - m)
    mx[...] = m
    sm[...] = jnp.sum(e, axis=0, keepdims=True)
    dl[...] = jnp.sum(e * grad_p, axis=0, keepdims=True)

    def take(j, keys, values):
        s, grad_p = scores_of(keys, values)
        sc[j] = s
        dp[j] = grad_p
        old = mx[...]
        m = jnp.maximum(old, jnp.max(s, axis=0, keepdims=True))
        e = jnp.exp(s - m)
        fix = jnp.exp(old - m)
        mx[...] = m
        sm[...] = sm[...] * fix + jnp.sum(e, axis=0, keepdims=True)
        dl[...] = dl[...] * fix + jnp.sum(e * grad_p, axis=0, keepdims=True)

    def take_chunk(j):
        @pl.when(j < z)
        def _():
            take(j, chunk_of(j, k_at), chunk_of(j, v_at))

    def ag_step(s, _):
        for blk in (h, g):
            ag_recv(0, s - 1, blk).wait_recv()
            ag_copy(0, s, blk).start()
            ag_recv(1, s - 1, blk).wait_recv()

            @pl.when(s < half - 1)
            def _():
                ag_copy(1, s, blk).start()

        take_chunk((z - s + nz) % nz)
        take_chunk((z + s) % nz)
        return 0

    lax.fori_loop(1, half, ag_step, 0)
    for blk in range(2):
        ag_recv(0, half - 1, blk).wait_recv()
    take_chunk((z + half) % nz)

    def take_prompt(i, _):
        take(n_resp_chunks + i, prompt_of(i, pk_at), prompt_of(i, pv_at))
        return 0

    lax.fori_loop(0, p_chunks, take_prompt, 0)

    inv = 1.0 / sm[...]
    sm[...] = inv
    dl[...] = dl[...] * inv
    dqt[...] = jnp.zeros_like(dqt)

    def give(j, keys):
        probs = (jnp.exp(sc[j] - mx[...]) * sm[...]).astype(BF16)
        grad_s = (probs.astype(F32) * (dp[j] - dl[...])).astype(BF16)
        d_values = jnp.dot(probs, gb[...].reshape(two, hd), preferred_element_type=F32)
        d_keys = jnp.dot(grad_s, qb[...].reshape(two, hd), preferred_element_type=F32) * scale
        dqt[...] += jnp.dot(keys.T, grad_s, preferred_element_type=F32)
        return d_keys.astype(BF16), d_values.astype(BF16)

    def give_prompt(i, _):
        d_keys, d_values = give(n_resp_chunks + i, prompt_of(i, pk_at))
        pp[pl.ds(i * per_chunk, per_chunk), :, pl.ds(0, prow), :] = d_keys.reshape(per_chunk, 2, prow, hd)
        pp[pl.ds(i * per_chunk, per_chunk), :, pl.ds(prow, prow), :] = d_values.reshape(per_chunk, 2, prow, hd)
        return 0

    lax.fori_loop(0, p_chunks, give_prompt, 0)

    def rs_chunk(d, s):
        return (z + half - s + nz) % nz if d == 0 else (z + half + 1 + s) % nz

    def give_chunk(j, dst):
        @pl.when(j <= z)
        def _():
            d_keys, d_values = give(j, chunk_of(j, k_at))
            dst[:, pl.ds(k_at, tok), :] = d_keys.reshape(2, tok, hd)
            dst[:, pl.ds(v_at, tok), :] = d_values.reshape(2, tok, hd)

        @pl.when(j > z)
        def _():
            dst[:, pl.ds(0, 2 * tok), :] = jnp.zeros((2, 2 * tok, hd), BF16)

        dst[:, pl.ds(pk_at, 2 * prow), :] = pp[j]

    def rs_first(d, blk):
        return remote(first.at[d, blk], rs.at[d, 0, blk], rs_s.at[d, 0, blk], rs_r.at[d, 0, blk], ring_to[d])

    def rs_in(d, s, blk):
        return remote(rs.at[d, s, blk], rs.at[d, s, blk], rs_s.at[d, s, blk], rs_r.at[d, s, blk], ring_to[d])

    def rs_next(d, s, blk):
        return remote(rs.at[d, s - 1, blk], rs.at[d, s, blk], rs_s.at[d, s, blk], rs_r.at[d, s, blk], ring_to[d])

    for d in range(2):
        give_chunk(rs_chunk(d, 0), first.at[d])
        for blk in range(2):
            rs_first(d, blk).start()
    for d in range(2):
        give_chunk(rs_chunk(d, 1), part.at[1, d])

    def rs_step(s, _):
        slot = s % 2
        for d in range(2):
            for blk in range(2):
                rs_in(d, s - 1, blk).wait_recv()
                total = rs[d, s - 1, blk].astype(F32) + part[slot, d, blk].astype(F32)
                rs[d, s - 1, blk] = total.astype(BF16)
                rs_next(d, s, blk).start()

        for d in range(2):
            give_chunk(rs_chunk(d, s + 1), part.at[1 - slot, d])
        return 0

    lax.fori_loop(1, half - 1, rs_step, 0)

    last = (half - 1) % 2
    d_q = (dqt[...] * scale).T.astype(BF16).reshape(2, rows, hd)
    dqs[...] = d_q
    gq_ref[h] = dqs[h]
    x_dq = remote(dqs.at[g], gq_ref.at[h], x_s.at[3], x_r.at[3], partner)
    x_dq_in = remote(dqs.at[g], gq_ref.at[g], x_s.at[3], x_r.at[3], partner)
    x_dq.start()

    for blk in range(2):
        rs_in(0, half - 2, blk).wait_recv()
        total = rs[0, half - 2, blk].astype(F32) + part[last, 0, blk].astype(F32)
        rs[0, half - 2, blk] = total.astype(BF16)
        rs_next(0, half - 1, blk).start()
    for blk in range(2):
        rs_in(1, half - 2, blk).wait_recv()
    for blk in range(2):
        rs_in(0, half - 1, blk).wait_recv()

    def final(blk):
        return (
            part[last, 1, blk].astype(F32) + rs[1, half - 2, blk].astype(F32) + rs[0, half - 1, blk].astype(F32)
        )

    other = final(g)
    fin[...] = other[: 2 * tok].astype(BF16)
    pother[...] = other[2 * tok :]
    x_p = remote(pother, pself.at[h], x_s.at[4], x_r.at[4], partner)
    x_p_in = remote(pother, pself.at[g], x_s.at[4], x_r.at[4], partner)
    x_p.start()
    x_f = remote(fin, xfin, x_s.at[5], x_r.at[5], partner)
    x_f.start()
    mine = final(h)
    grk_ref[h] = mine[:tok].astype(BF16)
    grv_ref[h] = mine[tok : 2 * tok].astype(BF16)
    pself[h] = mine[2 * tok :]
    x_p_in.wait_recv()
    pr[r] = pself[0] + pself[1]

    def p_copy(d):
        return remote(pr.at[r], pr.at[r], p_s.at[d], p_r.at[r], {"resp": (r + d) % nr})

    def p_in(d):
        src = (r + d) % nr
        return remote(pr.at[src], pr.at[src], p_s.at[d], p_r.at[src], {"resp": src})

    for d in range(1, nr):
        p_copy(d).start()
    x_f.wait_recv()
    grk_ref[g] = xfin[pl.ds(0, tok)]
    grv_ref[g] = xfin[pl.ds(tok, tok)]
    x_dq_in.wait_recv()
    for d in range(1, nr):
        p_in(d).wait_recv()
    total = pr[0]
    for i in range(1, nr):
        total = total + pr[i]
    gpk_ref[...] = total[:prow]
    gpv_ref[...] = total[prow:]

    for item in (x_kv, x_q, x_g, x_dq, x_p, x_f):
        item.wait_send()
    for d in range(1, nr):
        p_copy(d).wait_send()
    for d in range(2):
        for s in range(half if d == 0 else half - 1):
            for blk in range(2):
                ag_copy(d, s, blk).wait_send()
                rs_in(d, s, blk).wait_send()


def per_device(queries, prompt_keys, prompt_values, resp_keys, resp_values, upstream, behav_logp, cur_logp, advantages, lengths):
    members, tok, heads, hd = queries.shape
    nc = lax.axis_size("ctx")
    nr = lax.axis_size("resp")
    nz = nc // 2
    half = nz // 2
    prow = prompt_keys.shape[0]
    rows = tok * heads
    two = 2 * rows
    key_rows = 2 * tok
    blk = 2 * tok + 2 * prow
    slots = nz + (nc * prow) // key_rows
    vmem = pl.BlockSpec(memory_space=pltpu.VMEM)
    smem = pl.BlockSpec(memory_space=pltpu.SMEM)
    dma = pltpu.SemaphoreType.DMA
    outs = pl.pallas_call(
        functools.partial(kernel, nz=nz, nr=nr, tok=tok, heads=heads, prow=prow, full_len=tok * nc),
        name="grpo_backward",
        out_shape=(
            jax.ShapeDtypeStruct((members, rows, hd), BF16),
            jax.ShapeDtypeStruct((members, tok, hd), BF16),
            jax.ShapeDtypeStruct((members, tok, hd), BF16),
            jax.ShapeDtypeStruct((prow, hd), F32),
            jax.ShapeDtypeStruct((prow, hd), F32),
        ),
        in_specs=[vmem] * 8 + [smem] * 2,
        out_specs=(vmem,) * 5,
        scratch_shapes=[
            pltpu.VMEM((nz, 2, blk, hd), BF16),
            pltpu.VMEM((blk, hd), BF16),
            pltpu.VMEM((2, rows, hd), BF16),
            pltpu.VMEM((2, rows, hd), BF16),
            pltpu.VMEM((rows, hd), BF16),
            pltpu.VMEM((hd, two), BF16),
            pltpu.VMEM((hd, two), BF16),
            pltpu.VMEM((slots, key_rows, two), F32),
            pltpu.VMEM((slots, key_rows, two), F32),
            pltpu.VMEM((1, two), F32),
            pltpu.VMEM((1, two), F32),
            pltpu.VMEM((1, two), F32),
            pltpu.VMEM((hd, two), F32),
            pltpu.VMEM((nz, 2, 2 * prow, hd), BF16),
            pltpu.VMEM((2, 2, 2, blk, hd), BF16),
            pltpu.VMEM((2, 2, blk, hd), BF16),
            pltpu.VMEM((2, half, 2, blk, hd), BF16),
            pltpu.VMEM((2 * tok, hd), BF16),
            pltpu.VMEM((2 * tok, hd), BF16),
            pltpu.VMEM((2, rows, hd), BF16),
            pltpu.VMEM((2, 2 * prow, hd), F32),
            pltpu.VMEM((2 * prow, hd), F32),
            pltpu.VMEM((nr, 2 * prow, hd), F32),
            dma((2, half, 2)),
            dma((2, half, 2)),
            dma((2, half, 2)),
            dma((2, half, 2)),
            dma((6,)),
            dma((6,)),
            dma((nr,)),
            dma((nr,)),
        ],
        compiler_params=pltpu.CompilerParams(
            collective_id=0, has_side_effects=True, vmem_limit_bytes=48 * 1024 * 1024
        ),
    )(
        queries.reshape(members, rows, hd),
        upstream.reshape(members, rows, hd),
        prompt_keys, prompt_values, resp_keys, resp_values, behav_logp, cur_logp, advantages, lengths,
    )
    return (outs[0].reshape(queries.shape), *outs[1:])


def solution(mesh):
    placed = (
        P("resp", "ctx", None, None),
        P("ctx", None),
        P("ctx", None),
        P("resp", "ctx", None),
        P("resp", "ctx", None),
        P("resp", "ctx", None, None),
        P("resp", "ctx"),
        P("resp", "ctx"),
        P("resp"),
        P("resp"),
    )
    return jax.shard_map(
        per_device,
        mesh=mesh,
        in_specs=placed,
        out_specs=(
            P("resp", "ctx", None, None),
            P("resp", "ctx", None),
            P("resp", "ctx", None),
            P("ctx", None),
            P("ctx", None),
        ),
        check_vma=False,
    )
```

time: 1270 us -> 98.3 us (0.08); the launches traced: 1250 us -> 97.9 us
  waiting for transfers between devices: 1010 us -> 0 us
  blocking collectives: 190 us -> 0 us
  Pallas kernels: 0 us -> 88.6 us
  matrix products: 15.7 us -> 0 us
  between operations: 14.7 us -> 0.69 us
    reduce_scatter x1 -> x0, waiting for transfers between devices: 617 us -> none  [per_device(): lax.psum_scatter(summed.astype(jnp.bfloat16), 'ctx', scatter_dimension=0,...]
    unnamed x5 -> x0, waiting for transfers between devices: 245 us -> none
    all_gather x2 -> x0, waiting for transfers between devices: 147 us -> none  [the longest x1 137 us: per_device(): lax.all_gather(resp_values, 'ctx', axis=1, tiled=True)]
    all_gather x2 -> x0, blocking collectives: 128 us -> none  [the longest x1 69.9 us: per_device(): lax.all_gather(prompt_keys, 'ctx', axis=0, tiled=True)]
    pallas_call x0 -> x1, Pallas kernels: none -> 88.6 us  [per_device(): pl.pallas_call(functools.partial(kernel, nz=nz, nr=nr, tok=tok, heads=hea...]
    psum x1 -> x0, blocking collectives: 61.8 us -> none  [per_device(): prompt_total = lax.psum(ctx_share, 'resp')]
    dot_general x16 -> x0, matrix products: 15.7 us -> none  [the longest x4 3.86 us: member_term(): jnp.dot(score_cols.T, query_rows[member], preferred_element_type=jnp.floa...]
  transfers between devices with their start and end apart: 4 -> 0, of which waited for: 4 -> 0; matrix products, arithmetic and copies ran while one was open for 1% -> 0% of each run, Pallas kernels for 0% -> 0%
where the time goes in v1:
time: 98.3 us; the launch traced here: 97.9 us
  Pallas kernels  88.6 us (90%)
  local copies, waits for them, and re-layouts  8.6 us (9%)
    pallas_call x1, Pallas kernels, per_device(): pl.pallas_call(functools.partial(kernel, nz=nz, nr=nr, tok=tok, heads=hea...  88.6 us
    unnamed x25, local copies, waits for them, and re-layouts  8.6 us

profile of v1, /device:TPU:1, one launch (start us, length us, event | category | flops | bytes accessed | tf_op | source)
XLA Modules:
  0.0 97.9 jit_solution(4860551340801802111)
XLA Ops:
  0.6 0.0 copy-start.7
  0.6 0.0 copy-start.9
  0.7 0.0 copy-start.6
  0.7 0.0 copy-start.8
  0.7 0.6 copy-done.7
  1.3 0.0 copy-done.9
  1.3 0.0 copy-done.6
  1.3 0.0 copy-done.8
  1.3 0.0 copy-start
  1.4 0.9 copy-done
  2.3 0.0 copy-start.1
  2.3 0.9 copy-done.1
  3.3 0.0 copy-start.2
  3.3 0.8 copy-done.2
  4.0 0.0 copy-start.3
  4.0 0.8 copy-done.3
  4.8 0.0 copy-start.4
  4.8 0.7 copy-done.4
  5.5 0.0 copy-start.5
  5.5 0.7 copy-done.5
  6.1 88.6 %grpo_backward.1 = (bf16[2,512,128]{2,1,0:T(8,128)(2,1)S(1)}, bf16[2,64,128]{2,1,0:T(8,128)(2,1)S(1)}, bf16[2,64,128]{2,1,0:T(8,128)(2,1)S(1)}, f32[16,128]{1,0:T(8,128)S(1)}, f32[16,128]{1,0:T(8,128)S(1)}) custom-call(bf16[2,512,128]{2,1,0:T(8,128)(2,1)S(1)} %bitcast.3, bf16[2,512,128]{2,1,0:T(8,128)(2,1)S(1)} %bitcast.4, bf16[16,128]{1,0:T(8,128)(2,1)S(1)} %copy-done.4, ...), custom_call_target="tpu_custom_call" | custom-call | tf_op jit(solution)/shard_map/grpo_backward/pallas_call | solution.py:328
  94.8 0.7 copy.20
  95.5 0.6 copy.21
  96.1 0.6 copy.22
  96.7 0.6 copy.23
  97.3 0.6 copy.24
Async XLA Ops:
  0.6 0.7 copy-start.7
  0.6 0.7 copy-start.9
  0.7 0.7 copy-start.6
  0.7 0.7 copy-start.8
  1.3 1.0 copy-start
  2.3 0.9 copy-start.1
  3.3 0.8 copy-start.2
  4.0 0.8 copy-start.3
  4.8 0.7 copy-start.4
  5.5 0.7 copy-start.5

commit v2 on v1

v2 whole, which is shorter than its diff:
```python
import functools

import jax
import jax.numpy as jnp
from jax import lax
from jax.experimental import pallas as pl
from jax.experimental.pallas import tpu as pltpu
from jax.sharding import PartitionSpec as P

RATIO_CAP = 2.0
MESH = pl.DeviceIdType.MESH
F32 = jnp.float32
BF16 = jnp.bfloat16
LAST = (8, 7)
ORDER = (1, 4, 2, 5, 7, 3, 6, 8)
PARENT = {1: 0, 2: 1, 3: 2, 4: 0, 5: 4, 6: 5, 7: 4, 8: 7}
STAGE_A = ((0, 8), (0, 6), (1, 6), (1, 7), (0, 3), (1, 3))
STAGE_B = ((0, 7), (0, 5), (1, 5), (0, 2), (1, 2))
STAGE_C = ((0, 4), (1, 4), (0, 1), (1, 1), (0, 0))


def pick(i, values):
    n = len(values)
    total = 0
    for k, value in enumerate(values):
        if value:
            total = total + value * (1 - ((i + n - k) % n + n - 1) // n)
    return total


def remote(src, dst, ssem, rsem, dev):
    return pltpu.make_async_remote_copy(
        src_ref=src, dst_ref=dst, send_sem=ssem, recv_sem=rsem, device_id=dev, device_id_type=MESH
    )


def kernel(
    q_ref, u_ref, pk_ref, pv_ref, rk_ref, rv_ref, behav_ref, cur_ref, adv_ref, len_ref,
    gq_ref, grk_ref, grv_ref, gpk_ref, gpv_ref,
    kv, xkv, qb, ub, gb, gsend, behav, cur, adv, length_s, qt, gt, sc, dp, mx, sm, dl, dqt, dqs,
    part, rs, xself, pp, pc, ps, pz, pt, pr,
    in_s, ag_s, ag_r, rs_s, rs_r, x_s, x_r, pz_s, pz_r, pr_s, pr_r,
    *, nz, nr, tok, heads, prow, full_len,
):
    hd = q_ref.shape[-1]
    scale = hd ** (-0.5)
    rows = tok * heads
    two = 2 * rows
    key_rows = 2 * tok
    per_chunk = key_rows // (2 * prow)
    p_chunks = nz // per_chunk

    c = lax.axis_index("ctx")
    r = lax.axis_index("resp")
    z = c // 2
    h = c % 2
    g = 1 - h
    k = r % 2

    def at_z(off, col):
        return {"ctx": 2 * ((z + off + nz) % nz) + col}

    partner = {"ctx": 2 * z + g}
    other_core = {"resp": r + 1 - 2 * k}

    barrier = pltpu.get_barrier_semaphore()
    near = [partner, other_core]
    for off in (1, 4):
        for sign in (1, -1):
            near += [at_z(sign * off, h), at_z(sign * off, g)]
    near += [at_z(3, h), at_z(-3, h)]
    for dev in near:
        pl.semaphore_signal(barrier, 1, device_id=dev, device_id_type=MESH)

    def from_plane(i):
        return {"resp": (i // 2) * 2 + h, "ctx": 2 * z + i % 2}

    me = (r // 2) * 2 + h
    mine_too = (1 - (k + h) % 2)

    def greet(i, _):
        @pl.when(jnp.logical_or(i != me, k != h))
        def _():
            pl.semaphore_signal(barrier, 1, device_id=from_plane(i), device_id_type=MESH)

        return 0

    lax.fori_loop(0, nr, greet, 0)

    k_at, v_at, pk_at, pv_at = 0, tok, 2 * tok, 2 * tok + prow
    loads = [
        (rk_ref.at[h], kv.at[z, h, pl.ds(k_at, tok)]),
        (rv_ref.at[h], kv.at[z, h, pl.ds(v_at, tok)]),
        (pk_ref, kv.at[z, h, pl.ds(pk_at, prow)]),
        (pv_ref, kv.at[z, h, pl.ds(pv_at, prow)]),
        (rk_ref.at[g], xkv.at[pl.ds(k_at, tok)]),
        (rv_ref.at[g], xkv.at[pl.ds(v_at, tok)]),
        (pk_ref, xkv.at[pl.ds(pk_at, prow)]),
        (pv_ref, xkv.at[pl.ds(pv_at, prow)]),
        (len_ref, length_s),
        (adv_ref, adv),
        (behav_ref, behav),
        (cur_ref, cur),
        (u_ref, ub),
        (q_ref.at[h], qb.at[h]),
    ]
    loads = [pltpu.make_async_copy(src, dst, in_s.at[i]) for i, (src, dst) in enumerate(loads)]
    for load in loads:
        load.start()

    x_kv = remote(xkv, kv.at[z, h], x_s.at[0], x_r.at[0], partner)
    x_kv_in = remote(xkv, kv.at[z, g], x_s.at[0], x_r.at[0], partner)
    x_q = remote(q_ref.at[g], qb.at[h], x_s.at[1], x_r.at[1], partner)
    x_q_in = remote(q_ref.at[g], qb.at[g], x_s.at[1], x_r.at[1], partner)
    x_g = remote(gsend, gb.at[h], x_s.at[2], x_r.at[2], partner)
    x_g_in = remote(gsend, gb.at[g], x_s.at[2], x_r.at[2], partner)

    def down_from(d, o):
        return (z - o + nz) % nz if d == 0 else (z + o) % nz

    def sign(d):
        return 1 - 2 * d

    def ag_own(d, o, col):
        src = kv.at[z, h] if col is h else xkv
        return remote(src, kv.at[z, h], ag_s.at[d, o, col], ag_r.at[d, o, h], at_z(sign(d) * o, col))

    def ag_relay(d, o, hop, blk):
        chunk = down_from(d, o)
        return remote(
            kv.at[chunk, blk], kv.at[chunk, blk], ag_s.at[d, o + hop, blk], ag_r.at[d, o + hop, blk],
            at_z(sign(d) * hop, h),
        )

    def ag_in(d, o, blk):
        chunk = down_from(d, o)
        return remote(kv.at[chunk, blk], kv.at[chunk, blk], ag_s.at[d, o, blk], ag_r.at[d, o, blk], partner)

    for load in loads[:8]:
        load.wait()
    pl.semaphore_wait(barrier, len(near) + nr - mine_too)
    for o in (4, 1):
        for col in (g, h):
            for d in range(2):
                ag_own(d, o, col).start()
    x_kv.start()
    x_q.start()

    for load in loads[8:]:
        load.wait()
    row_of = lax.broadcasted_iota(jnp.int32, (rows, tok), 0) // heads
    col_of = lax.broadcasted_iota(jnp.int32, (rows, tok), 1)
    position = c * tok + lax.broadcasted_iota(jnp.int32, (1, tok), 1)

    def weighted(member):
        length = jnp.full((1, tok), length_s[member], jnp.int32)
        ratio = jnp.minimum(jnp.exp(cur[pl.ds(member, 1), :] - behav[pl.ds(member, 1), :]), RATIO_CAP)
        valid = (position < length).astype(F32)
        weight = -adv[member] * ratio * valid * (full_len / length.astype(F32))
        spread = jnp.where(row_of == col_of, jnp.broadcast_to(weight, (rows, tok)), 0.0)
        column = jnp.sum(spread, axis=1, keepdims=True)
        return (column * ub[member].astype(F32)).astype(BF16)

    gsend[...] = weighted(g)
    x_g.start()
    gb[h] = weighted(h)

    x_kv_in.wait_recv()
    x_q_in.wait_recv()
    qt[...] = qb[...].reshape(two, hd).T
    x_g_in.wait_recv()
    gt[...] = gb[...].reshape(two, hd).T

    def scores_of(keys, values):
        s = jnp.dot(keys, qt[...], preferred_element_type=F32) * scale
        return s, jnp.dot(values, gt[...], preferred_element_type=F32)

    def chunk_of(j, at):
        return kv[j, :, pl.ds(at, tok), :].reshape(key_rows, hd)

    def prompt_of(i, at):
        return kv[pl.ds(i * per_chunk, per_chunk), :, pl.ds(at, prow), :].reshape(key_rows, hd)

    s, grad_p = scores_of(chunk_of(z, k_at), chunk_of(z, v_at))
    key_pos = lax.broadcasted_iota(jnp.int32, (key_rows, two), 0)
    row_pos = lax.broadcasted_iota(jnp.int32, (key_rows, two), 1) // heads
    s = jnp.where(key_pos <= row_pos, s, -jnp.inf)
    sc[z] = s
    dp[z] = grad_p
    m = jnp.max(s, axis=0, keepdims=True)
    e = jnp.exp(s - m)
    mx[...] = m
    sm[...] = jnp.sum(e, axis=0, keepdims=True)
    dl[...] = jnp.sum(e * grad_p, axis=0, keepdims=True)

    def take(j, keys, values):
        s, grad_p = scores_of(keys, values)
        sc[j] = s
        dp[j] = grad_p
        old = mx[...]
        m = jnp.maximum(old, jnp.max(s, axis=0, keepdims=True))
        e = jnp.exp(s - m)
        fix = jnp.exp(old - m)
        mx[...] = m
        sm[...] = sm[...] * fix + jnp.sum(e, axis=0, keepdims=True)
        dl[...] = dl[...] * fix + jnp.sum(e * grad_p, axis=0, keepdims=True)

    def ag_step(i, _):
        o = pick(i, ORDER)
        for blk in (h, g):
            for d in range(2):

                @pl.when(o <= LAST[d])
                def _():
                    ag_in(d, o, blk).wait_recv()

                    @pl.when(jnp.logical_and(o % 3 != 0, o < LAST[d]))
                    def _():
                        ag_relay(d, o, 1, blk).start()

                    @pl.when(o == 4)
                    def _():
                        ag_relay(d, o, 3, blk).start()

        def one(d, _):
            j = (z + (2 * d - 1) * o + nz) % nz

            @pl.when(jnp.logical_and(j < z, o + d < 9))
            def _():
                take(j, chunk_of(j, k_at), chunk_of(j, v_at))

            return 0

        lax.fori_loop(0, 2, one, 0)
        return 0

    lax.fori_loop(0, len(ORDER), ag_step, 0)

    def take_prompt(i, _):
        take(nz + i, prompt_of(i, pk_at), prompt_of(i, pv_at))
        return 0

    lax.fori_loop(0, p_chunks, take_prompt, 0)

    inv = 1.0 / sm[...]
    sm[...] = inv
    dl[...] = dl[...] * inv
    dqt[...] = jnp.zeros_like(dqt)

    def give(j, keys):
        probs = (jnp.exp(sc[j] - mx[...]) * sm[...]).astype(BF16)
        grad_s = (probs.astype(F32) * (dp[j] - dl[...])).astype(BF16)
        d_values = jnp.dot(probs, gb[...].reshape(two, hd), preferred_element_type=F32)
        d_keys = jnp.dot(grad_s, qb[...].reshape(two, hd), preferred_element_type=F32) * scale
        dqt[...] += jnp.dot(keys.T, grad_s, preferred_element_type=F32)
        return d_keys.astype(BF16), d_values.astype(BF16)

    def give_at(d, o):
        j = (z + (2 * d - 1) * o + nz) % nz

        @pl.when(j <= z)
        def _():
            d_keys, d_values = give(j, chunk_of(j, k_at))
            part[d, o, :, pl.ds(k_at, tok), :] = d_keys.reshape(2, tok, hd)
            part[d, o, :, pl.ds(v_at, tok), :] = d_values.reshape(2, tok, hd)

        @pl.when(j > z)
        def _():
            part[d, o] = jnp.zeros((2, 2 * tok, hd), BF16)

    def rs_out(d, o, hop, blk):
        return remote(
            part.at[d, o, blk], rs.at[d, o, blk], rs_s.at[d, o, blk], rs_r.at[d, o, blk],
            {"ctx": 2 * ((z + (2 * d - 1) * hop + nz) % nz) + h},
        )

    def rs_root(d, o, col):
        return remote(
            part.at[d, o, col], rs.at[d, o, h], rs_s.at[d, o, col], rs_r.at[d, o, h], at_z(-sign(d) * o, col)
        )

    def rs_in(d, o, blk):
        return remote(rs.at[d, o, blk], rs.at[d, o, blk], rs_s.at[d, o, blk], rs_r.at[d, o, blk], partner)

    def stage_a(i, _):
        d = pick(i, [d for d, _ in STAGE_A])
        o = pick(i, [o for _, o in STAGE_A])
        hop = pick(i, [o - PARENT[o] for _, o in STAGE_A])
        give_at(d, o)
        for blk in range(2):
            rs_out(d, o, hop, blk).start()
        return 0

    lax.fori_loop(0, len(STAGE_A), stage_a, 0)

    def give_prompt(i, _):
        d_keys, d_values = give(nz + i, prompt_of(i, pk_at))
        d_keys = d_keys.reshape(per_chunk, 2, prow, hd)
        d_values = d_values.reshape(per_chunk, 2, prow, hd)
        for blk in range(2):
            pp[blk, pl.ds(i * per_chunk, per_chunk), pl.ds(0, prow), :] = d_keys[:, blk]
            pp[blk, pl.ds(i * per_chunk, per_chunk), pl.ds(prow, prow), :] = d_values[:, blk]
        return 0

    lax.fori_loop(0, p_chunks, give_prompt, 0)
    x_core = remote(pp.at[1 - k], pc, x_s.at[4], x_r.at[4], other_core)
    x_core.start()

    def stage_b(i, _):
        give_at(pick(i, [d for d, _ in STAGE_B]), pick(i, [o for _, o in STAGE_B]))
        return 0

    lax.fori_loop(0, len(STAGE_B), stage_b, 0)

    x_core.wait_recv()
    ps[...] = (pp[k].astype(F32) + pc[...].astype(F32)).astype(BF16)

    def pz_out(i):
        to = (z + i) % nz
        return remote(ps.at[to], pz.at[z], pz_s.at[i], pz_r.at[z], {"ctx": 2 * to + h})

    def pz_in(i):
        src = (z + i) % nz
        return remote(ps.at[src], pz.at[src], pz_s.at[i], pz_r.at[src], {"ctx": 2 * src + h})

    def send_pz(i, _):
        pz_out(i).start()
        return 0

    lax.fori_loop(1, nz, send_pz, 0)

    def join(d, o, children):
        for blk in range(2):
            for child in children:
                rs_in(d, child, blk).wait_recv()
            total = part[d, o, blk].astype(F32)
            for child in children:
                total = total + rs[d, child, blk].astype(F32)
            part[d, o, blk] = total.astype(BF16)
            if PARENT[o]:
                rs_out(d, o, o - PARENT[o], blk).start()
            else:
                rs_root(d, o, blk).start()

    for d, o in STAGE_B:
        join(d, o, [child for child in PARENT if PARENT[child] == o and child <= LAST[d]])

    def stage_c(i, _):
        give_at(pick(i, [d for d, _ in STAGE_C]), pick(i, [o for _, o in STAGE_C]))
        return 0

    lax.fori_loop(0, len(STAGE_C), stage_c, 0)

    x_own = remote(part.at[0, 0, g], xself, x_s.at[5], x_r.at[5], partner)
    x_own.start()

    for d, o in STAGE_C[:-1]:
        join(d, o, [child for child in PARENT if PARENT[child] == o and child <= LAST[d]])

    dqs[...] = (dqt[...] * scale).T.astype(BF16).reshape(2, rows, hd)
    x_dq = remote(dqs.at[g], gq_ref.at[h], x_s.at[3], x_r.at[3], partner)
    x_dq_in = remote(dqs.at[g], gq_ref.at[g], x_s.at[3], x_r.at[3], partner)
    x_dq.start()
    gq_ref[h] = dqs[h]

    def wait_pz(i, total):
        pz_in(i).wait_recv()
        return total + pz[(z + i) % nz].astype(F32)

    pt[...] = lax.fori_loop(1, nz, wait_pz, ps[z].astype(F32))

    def pr_out(i):
        return remote(pt, pr.at[me], pr_s.at[i], pr_r.at[me], {"resp": (r + i) % nr, "ctx": 2 * z + k})

    def pr_in(i):
        return remote(pt, pr.at[i], pr_s.at[i], pr_r.at[i], partner)

    @pl.when(k == h)
    def _():
        pr[me] = pt[...]

    def send_pr(i, _):
        @pl.when(jnp.logical_or(i != 0, k != h))
        def _():
            pr_out(i).start()

        return 0

    lax.fori_loop(0, nr, send_pr, 0)

    def total_of(own, member):
        total = own.astype(F32)
        for d, o in STAGE_C[:-1]:
            total = total + rs[d, o, member].astype(F32)
        return total.astype(BF16)

    x_own.wait_recv()
    for member in range(2):
        for d, o in STAGE_C[:-1]:
            rs_in(d, o, member).wait_recv()
    mine = total_of(part[0, 0, h], h)
    grk_ref[h] = mine[:tok]
    grv_ref[h] = mine[tok:]
    theirs = total_of(xself[...], g)
    grk_ref[g] = theirs[:tok]
    grv_ref[g] = theirs[tok:]

    def wait_pr(i, _):
        @pl.when(jnp.logical_or(i != me, k != h))
        def _():
            pr_in(i).wait_recv()

        return 0

    lax.fori_loop(0, nr, wait_pr, 0)
    total = pr[0]
    for i in range(1, nr):
        total = total + pr[i]
    gpk_ref[...] = total[:prow]
    gpv_ref[...] = total[prow:]
    x_dq_in.wait_recv()

    for item in (x_kv, x_q, x_g, x_dq, x_core, x_own):
        item.wait_send()
    for d in range(2):
        for o in range(1, LAST[d] + 1):
            for blk in range(2):
                ag_in(d, o, blk).wait_send()
                rs_in(d, o, blk).wait_send()

    def sent(i, _):
        @pl.when(i != 0)
        def _():
            pz_out(i).wait_send()

        @pl.when(jnp.logical_or(i != 0, k != h))
        def _():
            pr_out(i).wait_send()

        return 0

    lax.fori_loop(0, nr, sent, 0)


def write_out(*refs):
    n = len(refs) // 2
    sems = refs[-1]
    copies = [pltpu.make_async_copy(refs[i], refs[n + i], sems.at[i]) for i in range(n)]
    for copy in copies:
        copy.start()
    for copy in copies:
        copy.wait()


def per_device(queries, prompt_keys, prompt_values, resp_keys, resp_values, upstream, behav_logp, cur_logp, advantages, lengths):
    members, tok, heads, hd = queries.shape
    nc = lax.axis_size("ctx")
    nr = lax.axis_size("resp")
    nz = nc // 2
    prow = prompt_keys.shape[0]
    rows = tok * heads
    two = 2 * rows
    key_rows = 2 * tok
    blk = 2 * tok + 2 * prow
    slots = nz + (nc * prow) // key_rows
    vmem = pl.BlockSpec(memory_space=pltpu.VMEM)
    hbm = pl.BlockSpec(memory_space=pltpu.HBM)
    dma = pltpu.SemaphoreType.DMA
    offs = max(LAST) + 1
    shapes = (
        jax.ShapeDtypeStruct((members, rows, hd), BF16),
        jax.ShapeDtypeStruct((members, tok, hd), BF16),
        jax.ShapeDtypeStruct((members, tok, hd), BF16),
        jax.ShapeDtypeStruct((prow, hd), F32),
        jax.ShapeDtypeStruct((prow, hd), F32),
    )
    outs = pl.pallas_call(
        functools.partial(kernel, nz=nz, nr=nr, tok=tok, heads=heads, prow=prow, full_len=tok * nc),
        name="grpo_backward",
        out_shape=shapes,
        in_specs=[hbm] * 10,
        out_specs=(vmem,) * 5,
        scratch_shapes=[
            pltpu.VMEM((nz, 2, blk, hd), BF16),
            pltpu.VMEM((blk, hd), BF16),
            pltpu.VMEM((2, rows, hd), BF16),
            pltpu.VMEM((2, rows, hd), BF16),
            pltpu.VMEM((2, rows, hd), BF16),
            pltpu.VMEM((rows, hd), BF16),
            pltpu.VMEM((members, tok), F32),
            pltpu.VMEM((members, tok), F32),
            pltpu.SMEM((members,), F32),
            pltpu.SMEM((members,), jnp.int32),
            pltpu.VMEM((hd, two), BF16),
            pltpu.VMEM((hd, two), BF16),
            pltpu.VMEM((slots, key_rows, two), F32),
            pltpu.VMEM((slots, key_rows, two), F32),
            pltpu.VMEM((1, two), F32),
            pltpu.VMEM((1, two), F32),
            pltpu.VMEM((1, two), F32),
            pltpu.VMEM((hd, two), F32),
            pltpu.VMEM((2, rows, hd), BF16),
            pltpu.VMEM((2, offs, 2, 2 * tok, hd), BF16),
            pltpu.VMEM((2, offs, 2, 2 * tok, hd), BF16),
            pltpu.VMEM((2 * tok, hd), BF16),
            pltpu.VMEM((2, nz, 2 * prow, hd), BF16),
            pltpu.VMEM((nz, 2 * prow, hd), BF16),
            pltpu.VMEM((nz, 2 * prow, hd), BF16),
            pltpu.VMEM((nz, 2 * prow, hd), BF16),
            pltpu.VMEM((2 * prow, hd), F32),
            pltpu.VMEM((nr, 2 * prow, hd), F32),
            dma((14,)),
            dma((2, offs, 2)),
            dma((2, offs, 2)),
            dma((2, offs, 2)),
            dma((2, offs, 2)),
            dma((6,)),
            dma((6,)),
            dma((nz,)),
            dma((nz,)),
            dma((nr,)),
            dma((nr,)),
        ],
        compiler_params=pltpu.CompilerParams(
            collective_id=0, has_side_effects=True, vmem_limit_bytes=48 * 1024 * 1024
        ),
    )(
        queries.reshape(members, rows, hd),
        upstream.reshape(members, rows, hd),
        prompt_keys, prompt_values, resp_keys, resp_values, behav_logp, cur_logp, advantages, lengths,
    )
    outs = (outs[0].reshape(queries.shape), *outs[1:])
    return pl.pallas_call(
        write_out,
        name="write_out",
        out_shape=tuple(jax.ShapeDtypeStruct(o.shape, o.dtype) for o in outs),
        in_specs=[vmem] * 5,
        out_specs=(hbm,) * 5,
        scratch_shapes=[dma((5,))],
    )(*outs)


def solution(mesh):
    placed = (
        P("resp", "ctx", None, None),
        P("ctx", None),
        P("ctx", None),
        P("resp", "ctx", None),
        P("resp", "ctx", None),
        P("resp", "ctx", None, None),
        P("resp", "ctx"),
        P("resp", "ctx"),
        P("resp"),
        P("resp"),
    )
    return jax.shard_map(
        per_device,
        mesh=mesh,
        in_specs=placed,
        out_specs=(
            P("resp", "ctx", None, None),
            P("resp", "ctx", None),
            P("resp", "ctx", None),
            P("ctx", None),
            P("ctx", None),
        ),
        check_vma=False,
    )
```

time: 98.3 us -> 90.2 us (0.918)
  Pallas kernels: 88.6 us -> 80.6 us
    pallas_call x1, Pallas kernels: 88.6 us -> 78.8 us  [per_device(): pl.pallas_call(functools.partial(kernel, nz=nz, nr=nr, tok=tok, heads=hea...]
    pallas_call x0 -> x1, Pallas kernels: none -> 1.75 us  [per_device(): pl.pallas_call(write_out, name='write_out', out_shape=tuple((jax.ShapeDty...]
    unnamed x25 -> x30, local copies, waits for them, and re-layouts: 8.6 us -> 8.55 us
where the time goes in v2:
time: 90.2 us; the launch traced here: 89.8 us
  Pallas kernels  80.6 us (89%)
  local copies, waits for them, and re-layouts  8.55 us (9%)
    pallas_call x1, Pallas kernels, per_device(): pl.pallas_call(functools.partial(kernel, nz=nz, nr=nr, tok=tok, heads=hea...  78.8 us
    unnamed x30, local copies, waits for them, and re-layouts  8.55 us

profile of v2, /device:TPU:1, one launch (start us, length us, event | category | flops | bytes accessed | tf_op | source)
XLA Modules:
  0.0 89.8 jit_solution(5025945567285673512)
XLA Ops:
  0.6 0.0 copy-start.12
  0.6 0.0 copy-start.14
  0.7 0.0 copy-start.11
  0.7 0.0 copy-start.13
  0.7 0.6 copy-done.12
  1.3 0.0 copy-done.14
  1.3 0.0 copy-done.11
  1.3 0.0 copy-done.13
  1.3 0.0 copy-start
  1.4 0.9 %copy-done = bf16[2,64,8,128]{3,2,1,0:T(8,128)(2,1)S(1)} copy-done((bf16[2,64,8,128]{3,2,1,0:T(8,128)(2,1)S(1)}, bf16[2,64,8,128]{3,2,1,0:T(8,128)(2,1)}, u32[]{:S(2)}) %copy-start) | copy-done | bytes 262168
  2.3 0.0 copy-start.1
  2.3 0.9 %copy-done.1 = bf16[2,64,8,128]{3,2,1,0:T(8,128)(2,1)S(1)} copy-done((bf16[2,64,8,128]{3,2,1,0:T(8,128)(2,1)S(1)}, bf16[2,64,8,128]{3,2,1,0:T(8,128)(2,1)}, u32[]{:S(2)}) %copy-start.1) | copy-done | bytes 262168
  3.3 0.0 copy-start.3
  3.3 0.8 copy-done.3
  4.0 0.0 copy-start.4
  4.0 0.8 copy-done.4
  4.8 0.0 copy-start.9
  4.8 0.7 copy-done.9
  5.5 0.0 copy-start.10
  5.5 0.7 copy-done.10
  6.1 78.8 %grpo_backward.1 = (bf16[2,512,128]{2,1,0:T(8,128)(2,1)S(1)}, bf16[2,64,128]{2,1,0:T(8,128)(2,1)S(1)}, bf16[2,64,128]{2,1,0:T(8,128)(2,1)S(1)}, f32[16,128]{1,0:T(8,128)S(1)}, f32[16,128]{1,0:T(8,128)S(1)}) custom-call(bf16[2,512,128]{2,1,0:T(8,128)(2,1)S(1)} %bitcast.3, bf16[2,512,128]{2,1,0:T(8,128)(2,1)S(1)} %bitcast.4, bf16[16,128]{1,0:T(8,128)(2,1)S(1)} %copy-done.9, ...), custom_call_target="tpu_custom_call" | custom-call | tf_op jit(solution)/shard_map/grpo_backward/pallas_call | solution.py:477
  85.0 0.0 copy-start.2
  85.0 0.7 copy-done.2
  85.7 0.0 copy-start.5
  85.7 0.6 copy-done.5
  86.3 0.0 copy-start.6
  86.3 0.6 copy-done.6
  86.9 0.0 copy-start.7
  86.9 0.6 copy-done.7
  87.5 0.0 copy-start.8
  87.5 0.6 copy-done.8
  88.1 1.7 %write_out.1 = (bf16[2,64,8,128]{3,2,1,0:T(8,128)(2,1)}, bf16[2,64,128]{2,1,0:T(8,128)(2,1)}, bf16[2,64,128]{2,1,0:T(8,128)(2,1)}, f32[16,128]{1,0:T(8,128)}, f32[16,128]{1,0:T(8,128)}) custom-call(bf16[2,64,8,128]{3,2,1,0:T(8,128)(2,1)} %bitcast.5, bf16[2,64,128]{2,1,0:T(8,128)(2,1)} %copy-done.5, bf16[2,64,128]{2,1,0:T(8,128)(2,1)} %copy-done.6, ...), custom_call_target="tpu_custom_call" | custom-call | tf_op jit(solution)/shard_map/write_out/pallas_call | solution.py:533
Async XLA Ops:
  0.6 0.7 copy-start.12
  0.6 0.7 copy-start.14
  0.7 0.7 copy-start.11
  0.7 0.7 copy-start.13
  1.3 1.0 %copy-start = (bf16[2,64,8,128]{3,2,1,0:T(8,128)(2,1)S(1)}, bf16[2,64,8,128]{3,2,1,0:T(8,128)(2,1)}, u32[]{:S(2)}) copy-start(bf16[2,64,8,128]{3,2,1,0:T(8,128)(2,1)} %param.10) | copy-start | bytes 786436
  2.3 0.9 %copy-start.1 = (bf16[2,64,8,128]{3,2,1,0:T(8,128)(2,1)S(1)}, bf16[2,64,8,128]{3,2,1,0:T(8,128)(2,1)}, u32[]{:S(2)}) copy-start(bf16[2,64,8,128]{3,2,1,0:T(8,128)(2,1)} %param.15) | copy-start | bytes 786436
  3.3 0.8 copy-start.3
  4.0 0.8 copy-start.4
  4.8 0.7 copy-start.9
  5.5 0.7 copy-start.10
  85.0 0.7 copy-start.2
  85.7 0.6 copy-start.5
  86.3 0.6 copy-start.6
  86.9 0.6 copy-start.7
  87.5 0.6 copy-start.8

commit v3 on v2

v3 whole, which is shorter than its diff:
```python
import functools

import jax
import jax.numpy as jnp
from jax import lax
from jax.experimental import pallas as pl
from jax.experimental.pallas import tpu as pltpu
from jax.sharding import PartitionSpec as P

RATIO_CAP = 2.0
VMEM_BYTES = 63 * 1024 * 1024
MESH = pl.DeviceIdType.MESH
F32 = jnp.float32
BF16 = jnp.bfloat16
LAST = (8, 7)
ORDER = (1, 4, 2, 5, 7, 3, 6, 8)
PARENT = {1: 0, 2: 1, 3: 2, 4: 0, 5: 4, 6: 5, 7: 4, 8: 7}
STAGE_A = ((0, 8), (0, 6), (1, 6), (1, 7), (0, 3), (1, 3))
STAGE_B = ((0, 7), (0, 5), (1, 5), (0, 2), (1, 2))
STAGE_C = ((0, 4), (1, 4), (0, 1), (1, 1), (0, 0))
ROOTS = ((0, 4), (1, 4), (0, 1), (1, 1))
FIRST = (4, 3, 1)
THEN = {4: (8, 7, 5), 3: (6,), 1: (2,)}


def pick(i, values):
    n = len(values)
    total = i * 0
    for k, value in enumerate(values):
        if value:
            total = total + value * (1 - ((i + n - k) % n + n - 1) // n)
    return total


def reach(o):
    return max([o] + [reach(child) for child in PARENT if PARENT[child] == o and child <= LAST[1]])


def children(d, o):
    return [child for child in PARENT if PARENT[child] == o and child <= LAST[d]]


def remote(src, dst, ssem, rsem, dev):
    return pltpu.make_async_remote_copy(
        src_ref=src, dst_ref=dst, send_sem=ssem, recv_sem=rsem, device_id=dev, device_id_type=MESH
    )


def kernel(
    q_ref, u_ref, pk_ref, pv_ref, rk_ref, rv_ref, behav_ref, cur_ref, adv_ref, len_ref,
    gq_ref, grk_ref, grv_ref, gpk_ref, gpv_ref,
    kv, xkv, own_p, pkv, qb, ub, gb, gsend, behav, cur, adv, length_s, qt, gt, sc, dp, mx, sm, dl, dqt, dqs,
    part, rs, xself, pp, pc, pt, pz, pf,
    in_s, ag_s, ag_r, rs_s, rs_r, x_s, x_r, pm_s, pm_r, pl_s, pl_r, pa_s, pa_r, pz_s, pz_r, pf_s, pf_r,
    *, nz, nr, tok, heads, prow, full_len,
):
    hd = q_ref.shape[-1]
    scale = hd ** (-0.5)
    rows = tok * heads
    two = 2 * rows
    key_rows = 2 * tok
    shards = 2 * nr
    per_chunk = key_rows // prow
    p_chunks = shards // per_chunk

    r = lax.axis_index("resp")
    c = lax.axis_index("ctx")
    z = c // 2
    h = c % 2
    g = 1 - h
    p = 2 * r + h

    def at_z(off, col):
        return {"ctx": 2 * ((z + off + nz) % nz) + col}

    def in_plane(i):
        q = (p + i) % shards
        return q, {"resp": q // 2, "ctx": 2 * z + q % 2}

    partner = {"ctx": 2 * z + g}

    loads = [
        (rk_ref.at[g], xkv.at[pl.ds(0, tok)]),
        (rv_ref.at[g], xkv.at[pl.ds(tok, tok)]),
        (rk_ref.at[h], kv.at[z, h, pl.ds(0, tok)]),
        (rv_ref.at[h], kv.at[z, h, pl.ds(tok, tok)]),
        (pk_ref, own_p.at[pl.ds(0, prow)]),
        (pv_ref, own_p.at[pl.ds(prow, prow)]),
        (len_ref, length_s),
        (adv_ref, adv),
        (behav_ref, behav),
        (cur_ref, cur),
        (u_ref, ub),
        (q_ref.at[h], qb.at[h]),
    ]
    loads = [pltpu.make_async_copy(src, dst, in_s.at[i]) for i, (src, dst) in enumerate(loads)]
    for load in loads:
        load.start()

    barrier = pltpu.get_barrier_semaphore()
    for hop in (4, 3, 1):
        for way in (1, -1):
            pl.semaphore_signal(barrier, 1, device_id=at_z(way * hop, h), device_id_type=MESH)

    def greet(i, _):
        pl.semaphore_signal(barrier, 1, device_id=in_plane(i)[1], device_id_type=MESH)
        return 0

    lax.fori_loop(1, shards, greet, 0)
    x_kv = remote(xkv, kv.at[z, h], x_s.at[0], x_r.at[0], partner)
    x_kv_in = remote(xkv, kv.at[z, g], x_s.at[0], x_r.at[0], partner)
    x_q = remote(q_ref.at[g], qb.at[h], x_s.at[1], x_r.at[1], partner)
    x_q_in = remote(q_ref.at[g], qb.at[g], x_s.at[1], x_r.at[1], partner)
    x_g = remote(gsend, gb.at[h], x_s.at[2], x_r.at[2], partner)
    x_g_in = remote(gsend, gb.at[g], x_s.at[2], x_r.at[2], partner)

    def chunk_at(d, o):
        return (z + (2 * d - 1) * o + nz) % nz

    def edge_in(d, o, far):
        return z >= o if d == 0 else chunk_at(1, o) < far

    def edge_out(d, o, child, far):
        if d == 0:
            return jnp.logical_and(z >= o, z + child - o < nz)
        return chunk_at(1, o) < far

    def ag_out(d, o, child, blk):
        chunk = chunk_at(d, o)
        return remote(
            kv.at[chunk, blk], kv.at[chunk, blk], ag_s.at[d, child, blk], ag_r.at[d, child, blk],
            at_z((1 - 2 * d) * (child - o), h),
        )

    def ag_in(d, o, blk):
        chunk = chunk_at(d, o)
        return remote(kv.at[chunk, blk], kv.at[chunk, blk], ag_s.at[d, o, blk], ag_r.at[d, o, blk], partner)

    def ag_send(d, o, child, far, blk):
        @pl.when(edge_out(d, o, child, far))
        def _():
            ag_out(d, o, child, blk).start()

    ahead = (z - r + nz) % nz

    def pm_out(d, o, child):
        return remote(pkv.at[p], pkv.at[p], pm_s.at[d, child], pm_r.at[0], at_z((1 - 2 * d) * (child - o), h))

    def pm_at(d, o):
        return ahead == (o if d == 0 else nz - o)

    def pl_out(i):
        return remote(pkv.at[p], pkv.at[p], pl_s.at[i], pl_r.at[p], in_plane(i)[1])

    def pl_in(i):
        q, dev = in_plane(i)
        return remote(pkv.at[q], pkv.at[q], pl_s.at[i], pl_r.at[q], dev)

    def send_plane():
        def one(i, _):
            pl_out(i).start()
            return 0

        lax.fori_loop(1, shards, one, 0)

    for load in loads[:6]:
        load.wait()
    pl.semaphore_wait(barrier, 6 + shards - 1)
    x_kv.start()
    for d, o in ROOTS:
        ag_send(d, 0, o, reach(o), h)
    x_q.start()

    @pl.when(z == r)
    def _():
        pkv[p] = own_p[...]
        for o in FIRST:
            for d in range(2):
                pm_out(d, 0, o).start()

    row_of = lax.broadcasted_iota(jnp.int32, (rows, tok), 0) // heads
    col_of = lax.broadcasted_iota(jnp.int32, (rows, tok), 1)

    position = c * tok + lax.broadcasted_iota(jnp.int32, (1, tok), 1)
    for load in loads[6:]:
        load.wait()

    def weighted(member):
        length = jnp.full((1, tok), length_s[member], jnp.int32)
        ratio = jnp.minimum(jnp.exp(cur[pl.ds(member, 1), :] - behav[pl.ds(member, 1), :]), RATIO_CAP)
        valid = (position < length).astype(F32)
        weight = -adv[member] * ratio * valid * (full_len / length.astype(F32))
        spread = jnp.where(row_of == col_of, jnp.broadcast_to(weight, (rows, tok)), 0.0)
        column = jnp.sum(spread, axis=1, keepdims=True)
        return (column * ub[member].astype(F32)).astype(BF16)

    gsend[...] = weighted(g)
    x_g.start()

    @pl.when(z == r)
    def _():
        send_plane()

    gb[h] = weighted(h)
    x_kv_in.wait_recv()
    for d, o in ROOTS:
        ag_send(d, 0, o, reach(o), g)

    def ag_step(i):
        o = pick(i, ORDER)
        far = pick(i, [reach(o) if o <= LAST[1] else 0 for o in ORDER])
        far_next = pick(i, [reach(o + 1) if o + 1 in children(1, o) else 0 for o in ORDER])
        for blk in (h, g):
            for d in range(2):

                @pl.when(edge_in(d, o, far))
                def _():
                    ag_in(d, o, blk).wait_recv()

                    @pl.when(o == 4)
                    def _():
                        ag_send(d, 4, 7, reach(7), blk)

                    @pl.when(jnp.logical_and(o % 3 != 0, o < LAST[d]))
                    def _():
                        ag_send(d, o, o + 1, far_next, blk)

    def is_first():
        at = [pm_at(d, o) for d in range(2) for o in FIRST]
        return functools.reduce(jnp.logical_or, at)

    def pm_first():
        @pl.when(is_first())
        def _():
            pm_out(0, 0, 1).wait_recv()
            for d in range(2):
                for o in FIRST:

                    @pl.when(pm_at(d, o))
                    def _():
                        for child in THEN[o]:
                            if child <= LAST[d]:
                                pm_out(d, o, child).start()

            send_plane()

    def pm_then():
        @pl.when(jnp.logical_not(jnp.logical_or(is_first(), ahead == 0)))
        def _():
            pm_out(0, 0, 1).wait_recv()
            send_plane()

    def scores_of(keys, values):
        s = jnp.dot(keys, qt[...], preferred_element_type=F32) * scale
        return s, jnp.dot(values, gt[...], preferred_element_type=F32)

    def chunk_of(j, at):
        return kv[j, :, pl.ds(at, tok), :].reshape(key_rows, hd)

    def prompt_of(i, at):
        return pkv[pl.ds(i * per_chunk, per_chunk), pl.ds(at, prow), :].reshape(key_rows, hd)

    def take(j, keys, values):
        s, grad_p = scores_of(keys, values)
        sc[j] = s
        dp[j] = grad_p
        old = mx[...]
        m = jnp.maximum(old, jnp.max(s, axis=0, keepdims=True))
        e = jnp.exp(s - m)
        fix = jnp.exp(old - m)
        mx[...] = m
        sm[...] = sm[...] * fix + jnp.sum(e, axis=0, keepdims=True)
        dl[...] = dl[...] * fix + jnp.sum(e * grad_p, axis=0, keepdims=True)

    def take_pair(i):
        o = pick(i, ORDER)

        def one(d, _):
            j = chunk_at(d, o)

            @pl.when(jnp.logical_and(j < z, o + d < 9))
            def _():
                take(j, chunk_of(j, 0), chunk_of(j, tok))

            return 0

        lax.fori_loop(0, 2, one, 0)

    def early(i, _):
        ag_step(i)
        return 0

    ag_step(jnp.int32(0))
    pm_first()
    lax.fori_loop(1, 3, early, 0)
    pm_then()

    x_q_in.wait_recv()
    qt[...] = qb[...].reshape(two, hd).T
    x_g_in.wait_recv()
    gt[...] = gb[...].reshape(two, hd).T
    s, grad_p = scores_of(chunk_of(z, 0), chunk_of(z, tok))
    key_pos = lax.broadcasted_iota(jnp.int32, (key_rows, two), 0)
    row_pos = lax.broadcasted_iota(jnp.int32, (key_rows, two), 1) // heads
    s = jnp.where(key_pos <= row_pos, s, -jnp.inf)
    sc[z] = s
    dp[z] = grad_p
    m = jnp.max(s, axis=0, keepdims=True)
    e = jnp.exp(s - m)
    mx[...] = m
    sm[...] = jnp.sum(e, axis=0, keepdims=True)
    dl[...] = jnp.sum(e * grad_p, axis=0, keepdims=True)

    def behind(i, _):
        @pl.when(i > 2)
        def _():
            ag_step(i)

        take_pair(i)
        return 0

    lax.fori_loop(0, len(ORDER), behind, 0)

    def wait_plane(i, _):
        pl_in(i).wait_recv()
        return 0

    lax.fori_loop(1, shards, wait_plane, 0)

    def take_prompt(i, _):
        take(nz + i, prompt_of(i, 0), prompt_of(i, prow))
        return 0

    lax.fori_loop(0, p_chunks, take_prompt, 0)

    inv = 1.0 / sm[...]
    sm[...] = inv
    dl[...] = dl[...] * inv
    dqt[...] = jnp.zeros_like(dqt)

    def give(j, keys):
        probs = (jnp.exp(sc[j] - mx[...]) * sm[...]).astype(BF16)
        grad_s = (probs.astype(F32) * (dp[j] - dl[...])).astype(BF16)
        d_values = jnp.dot(probs, gb[...].reshape(two, hd), preferred_element_type=F32)
        d_keys = jnp.dot(grad_s, qb[...].reshape(two, hd), preferred_element_type=F32) * scale
        dqt[...] += jnp.dot(keys.T, grad_s, preferred_element_type=F32)
        return d_keys.astype(BF16), d_values.astype(BF16)

    def pa_out(i):
        q, dev = in_plane(i)
        return remote(pp.at[q], pc.at[p], pa_s.at[i], pa_r.at[p], dev)

    def pa_in(i):
        q, dev = in_plane(i)
        return remote(pp.at[q], pc.at[q], pa_s.at[i], pa_r.at[q], dev)

    def give_prompt(i, _):
        d_keys, d_values = give(nz + i, prompt_of(i, 0))
        pp[pl.ds(i * per_chunk, per_chunk), pl.ds(0, prow), :] = d_keys.reshape(per_chunk, prow, hd)
        pp[pl.ds(i * per_chunk, per_chunk), pl.ds(prow, prow), :] = d_values.reshape(per_chunk, prow, hd)
        return 0

    lax.fori_loop(0, p_chunks, give_prompt, 0)

    def send_pa(i, _):
        pa_out(i).start()
        return 0

    lax.fori_loop(1, shards, send_pa, 0)

    def give_at(d, o):
        j = chunk_at(d, o)

        @pl.when(j <= z)
        def _():
            d_keys, d_values = give(j, chunk_of(j, 0))
            part[d, o, :, pl.ds(0, tok), :] = d_keys.reshape(2, tok, hd)
            part[d, o, :, pl.ds(tok, tok), :] = d_values.reshape(2, tok, hd)

        @pl.when(j > z)
        def _():
            part[d, o] = jnp.zeros((2, 2 * tok, hd), BF16)

    def rs_out(d, o, hop, blk):
        return remote(
            part.at[d, o, blk], rs.at[d, o, blk], rs_s.at[d, o, blk], rs_r.at[d, o, blk], at_z((2 * d - 1) * hop, h)
        )

    def rs_root(d, o, col):
        return remote(
            part.at[d, o, col], rs.at[d, o, h], rs_s.at[d, o, col], rs_r.at[d, o, h], at_z((2 * d - 1) * o, col)
        )

    def rs_in(d, o, blk):
        return remote(rs.at[d, o, blk], rs.at[d, o, blk], rs_s.at[d, o, blk], rs_r.at[d, o, blk], partner)

    def stage_a(i, _):
        d = pick(i, [d for d, _ in STAGE_A])
        o = pick(i, [o for _, o in STAGE_A])
        hop = pick(i, [o - PARENT[o] for _, o in STAGE_A])
        far = pick(i, [reach(o) if d else 0 for d, o in STAGE_A])
        give_at(d, o)

        @pl.when(jnp.logical_or(jnp.logical_and(d == 0, z >= o), jnp.logical_and(d == 1, chunk_at(1, o) < far)))
        def _():
            for blk in range(2):
                rs_out(d, o, hop, blk).start()

        return 0

    lax.fori_loop(0, len(STAGE_A), stage_a, 0)

    def stage_b(i, _):
        give_at(pick(i, [d for d, _ in STAGE_B]), pick(i, [o for _, o in STAGE_B]))
        return 0

    lax.fori_loop(0, len(STAGE_B), stage_b, 0)

    def join(d, o):
        @pl.when(edge_in(d, o, reach(o)))
        def _():
            for blk in range(2):
                for child in children(d, o):

                    @pl.when(edge_out(d, o, child, reach(child)))
                    def _():
                        rs_in(d, child, blk).wait_recv()
                        part[d, o, blk] = (part[d, o, blk].astype(F32) + rs[d, child, blk].astype(F32)).astype(BF16)

                if PARENT[o]:
                    rs_out(d, o, o - PARENT[o], blk).start()
                else:
                    rs_root(d, o, blk).start()

    for d, o in STAGE_B:
        join(d, o)

    def wait_pa(i, total):
        pa_in(i).wait_recv()
        return total + pc[(p + i) % shards].astype(F32)

    pt[...] = lax.fori_loop(1, shards, wait_pa, pp[p].astype(F32))
    pz_out = remote(pt, pz.at[z], pz_s.at[0], pz_r.at[z], at_z(r - z, h))

    @pl.when(z != r)
    def _():
        pz_out.start()

    def stage_c(i, _):
        give_at(pick(i, [d for d, _ in STAGE_C]), pick(i, [o for _, o in STAGE_C]))
        return 0

    lax.fori_loop(0, len(STAGE_C), stage_c, 0)

    x_own = remote(part.at[0, 0, g], xself, x_s.at[4], x_r.at[4], partner)
    x_own.start()

    for d, o in ROOTS:
        join(d, o)

    dqs[...] = (dqt[...] * scale).T.astype(BF16).reshape(2, rows, hd)
    x_dq = remote(dqs.at[g], gq_ref.at[h], x_s.at[3], x_r.at[3], partner)
    x_dq_in = remote(dqs.at[g], gq_ref.at[g], x_s.at[3], x_r.at[3], partner)
    x_dq.start()
    gq_ref[h] = dqs[h]

    def pf_out(i):
        return remote(pf, pf, pf_s.at[i], pf_r.at[0], {"resp": (r + i) % nr})

    @pl.when(z == r)
    def _():
        def wait_pz(i, total):
            src = (z + i) % nz
            remote(pt, pz.at[src], pz_s.at[0], pz_r.at[src], partner).wait_recv()
            return total + pz[src]

        pf[...] = lax.fori_loop(1, nz, wait_pz, pt[...])

        def send_pf(i, _):
            pf_out(i).start()
            return 0

        lax.fori_loop(1, nr, send_pf, 0)

    def total_of(own, member):
        total = own.astype(F32)
        for d, o in ROOTS:
            total = total + rs[d, o, member].astype(F32)
        return total.astype(BF16)

    for member in range(2):
        for d, o in ROOTS:
            used = edge_out(d, 0, o, reach(o))

            @pl.when(used)
            def _():
                rs_in(d, o, member).wait_recv()

            @pl.when(jnp.logical_not(used))
            def _():
                rs[d, o, member] = jnp.zeros((2 * tok, hd), BF16)

    mine = total_of(part[0, 0, h], h)
    grk_ref[h] = mine[:tok]
    grv_ref[h] = mine[tok:]
    x_own.wait_recv()
    theirs = total_of(xself[...], g)
    grk_ref[g] = theirs[:tok]
    grv_ref[g] = theirs[tok:]

    for item in (x_kv, x_q, x_g, x_dq, x_own):
        item.wait_send()
    for d in range(2):
        for o in range(1, LAST[d] + 1):

            @pl.when(edge_out(d, PARENT[o], o, reach(o) if d else 0))
            def _():
                for blk in range(2):
                    ag_in(d, o, blk).wait_send()

            @pl.when(edge_in(d, o, reach(o) if d else 0))
            def _():
                for blk in range(2):
                    rs_in(d, o, blk).wait_send()


    for d in range(2):
        for o in FIRST:

            @pl.when(ahead == 0)
            def _():
                pm_out(d, 0, o).wait_send()

            @pl.when(pm_at(d, o))
            def _():
                for child in THEN[o]:
                    if child <= LAST[d]:
                        pm_out(d, o, child).wait_send()

    def sent(i, _):
        pl_out(i).wait_send()
        pa_out(i).wait_send()
        return 0

    lax.fori_loop(1, shards, sent, 0)

    x_dq_in.wait_recv()

    @pl.when(z != r)
    def _():
        pz_out.wait_send()
        pf_out(0).wait_recv()

    @pl.when(z == r)
    def _():
        def sent_pf(i, _):
            pf_out(i).wait_send()
            return 0

        lax.fori_loop(1, nr, sent_pf, 0)

    gpk_ref[...] = pf[:prow]
    gpv_ref[...] = pf[prow:]


def write_out(*refs):
    n = len(refs) // 2
    sems = refs[-1]
    copies = [pltpu.make_async_copy(refs[i], refs[n + i], sems.at[i]) for i in range(n)]
    for copy in copies:
        copy.start()
    for copy in copies:
        copy.wait()


def per_device(queries, prompt_keys, prompt_values, resp_keys, resp_values, upstream, behav_logp, cur_logp, advantages, lengths):
    members, tok, heads, hd = queries.shape
    nc = lax.axis_size("ctx")
    nr = lax.axis_size("resp")
    nz = nc // 2
    prow = prompt_keys.shape[0]
    rows = tok * heads
    two = 2 * rows
    key_rows = 2 * tok
    shards = 2 * nr
    slots = nz + (nc * prow) // key_rows
    vmem = pl.BlockSpec(memory_space=pltpu.VMEM)
    hbm = pl.BlockSpec(memory_space=pltpu.HBM)
    dma = pltpu.SemaphoreType.DMA
    offs = max(LAST) + 1
    shapes = (
        jax.ShapeDtypeStruct((members, rows, hd), BF16),
        jax.ShapeDtypeStruct((members, tok, hd), BF16),
        jax.ShapeDtypeStruct((members, tok, hd), BF16),
        jax.ShapeDtypeStruct((prow, hd), F32),
        jax.ShapeDtypeStruct((prow, hd), F32),
    )
    outs = pl.pallas_call(
        functools.partial(kernel, nz=nz, nr=nr, tok=tok, heads=heads, prow=prow, full_len=tok * nc),
        name="grpo_backward",
        out_shape=shapes,
        in_specs=[hbm] * 10,
        out_specs=(vmem,) * 5,
        scratch_shapes=[
            pltpu.VMEM((nz, 2, 2 * tok, hd), BF16),
            pltpu.VMEM((2 * tok, hd), BF16),
            pltpu.VMEM((2 * prow, hd), BF16),
            pltpu.VMEM((shards, 2 * prow, hd), BF16),
            pltpu.VMEM((2, rows, hd), BF16),
            pltpu.VMEM((2, rows, hd), BF16),
            pltpu.VMEM((2, rows, hd), BF16),
            pltpu.VMEM((rows, hd), BF16),
            pltpu.VMEM((members, tok), F32),
            pltpu.VMEM((members, tok), F32),
            pltpu.SMEM((members,), F32),
            pltpu.SMEM((members,), jnp.int32),
            pltpu.VMEM((hd, two), BF16),
            pltpu.VMEM((hd, two), BF16),
            pltpu.VMEM((slots, key_rows, two), F32),
            pltpu.VMEM((slots, key_rows, two), F32),
            pltpu.VMEM((1, two), F32),
            pltpu.VMEM((1, two), F32),
            pltpu.VMEM((1, two), F32),
            pltpu.VMEM((hd, two), F32),
            pltpu.VMEM((2, rows, hd), BF16),
            pltpu.VMEM((2, offs, 2, 2 * tok, hd), BF16),
            pltpu.VMEM((2, offs, 2, 2 * tok, hd), BF16),
            pltpu.VMEM((2 * tok, hd), BF16),
            pltpu.VMEM((shards, 2 * prow, hd), BF16),
            pltpu.VMEM((shards, 2 * prow, hd), BF16),
            pltpu.VMEM((2 * prow, hd), F32),
            pltpu.VMEM((nz, 2 * prow, hd), F32),
            pltpu.VMEM((2 * prow, hd), F32),
            dma((12,)),
            dma((2, offs, 2)),
            dma((2, offs, 2)),
            dma((2, offs, 2)),
            dma((2, offs, 2)),
            dma((5,)),
            dma((5,)),
            dma((2, offs)),
            dma((1,)),
            dma((shards,)),
            dma((shards,)),
            dma((shards,)),
            dma((shards,)),
            dma((1,)),
            dma((nz,)),
            dma((nr,)),
            dma((1,)),
        ],
        compiler_params=pltpu.CompilerParams(
            collective_id=0, has_side_effects=True, vmem_limit_bytes=VMEM_BYTES
        ),
    )(
        queries.reshape(members, rows, hd),
        upstream.reshape(members, rows, hd),
        prompt_keys, prompt_values, resp_keys, resp_values, behav_logp, cur_logp, advantages, lengths,
    )
    outs = (outs[0].reshape(queries.shape), *outs[1:])
    return pl.pallas_call(
        write_out,
        name="write_out",
        out_shape=tuple(jax.ShapeDtypeStruct(o.shape, o.dtype) for o in outs),
        in_specs=[vmem] * 5,
        out_specs=(hbm,) * 5,
        scratch_shapes=[dma((5,))],
        compiler_params=pltpu.CompilerParams(vmem_limit_bytes=VMEM_BYTES),
    )(*outs)


def solution(mesh):
    placed = (
        P("resp", "ctx", None, None),
        P("ctx", None),
        P("ctx", None),
        P("resp", "ctx", None),
        P("resp", "ctx", None),
        P("resp", "ctx", None, None),
        P("resp", "ctx"),
        P("resp", "ctx"),
        P("resp"),
        P("resp"),
    )
    return jax.shard_map(
        per_device,
        mesh=mesh,
        in_specs=placed,
        out_specs=(
            P("resp", "ctx", None, None),
            P("resp", "ctx", None),
            P("resp", "ctx", None),
            P("ctx", None),
            P("ctx", None),
        ),
        check_vma=False,
    )
```

time: 90.2 us -> 70.9 us (0.79)
  the two profiles are of different devices: /device:TPU:1 before, /device:TPU:27 now
where the time goes in v3:
time: 70.9 us; the launch traced here: 70.8 us
  Pallas kernels  70.1 us (99%)
    pallas_call x1, Pallas kernels, per_device(): pl.pallas_call(functools.partial(kernel, nz=nz, nr=nr, tok=tok, heads=hea...  68.4 us
    pallas_call x1, Pallas kernels, per_device(): pl.pallas_call(write_out, name='write_out', out_shape=tuple((jax.ShapeDty...  1.75 us

profile of v3, /device:TPU:27, one launch (start us, length us, event | category | flops | bytes accessed | tf_op | source)
XLA Modules:
  0.0 70.8 jit_solution(2741102405473017393)
XLA Ops:
  0.6 68.4 %grpo_backward.1 = (bf16[2,512,128]{2,1,0:T(8,128)(2,1)}, bf16[2,64,128]{2,1,0:T(8,128)(2,1)}, bf16[2,64,128]{2,1,0:T(8,128)(2,1)}, f32[16,128]{1,0:T(8,128)}, f32[16,128]{1,0:T(8,128)}) custom-call(bf16[2,512,128]{2,1,0:T(8,128)(2,1)} %bitcast.3, bf16[2,512,128]{2,1,0:T(8,128)(2,1)} %bitcast.4, bf16[16,128]{1,0:T(8,128)(2,1)} %pk_ref.1, ...), custom_call_target="tpu_custom_call" | custom-call | tf_op jit(solution)/shard_map/grpo_backward/pallas_call | solution.py:598
  69.0 1.8 %write_out.1 = (bf16[2,64,8,128]{3,2,1,0:T(8,128)(2,1)}, bf16[2,64,128]{2,1,0:T(8,128)(2,1)}, bf16[2,64,128]{2,1,0:T(8,128)(2,1)}, f32[16,128]{1,0:T(8,128)}, f32[16,128]{1,0:T(8,128)}) custom-call(bf16[2,64,8,128]{3,2,1,0:T(8,128)(2,1)} %bitcast.5, bf16[2,64,128]{2,1,0:T(8,128)(2,1)} %get-tuple-element.11.refs_1_, ...), custom_call_target="tpu_custom_call" | custom-call | tf_op jit(solution)/shard_map/write_out/pallas_call | solution.py:661

commit v4 on v3

--- a/solution.py
+++ b/solution.py
@@ -455,14 +455,14 @@
     x_own = remote(part.at[0, 0, g], xself, x_s.at[4], x_r.at[4], partner)
     x_own.start()
 
-    for d, o in ROOTS:
-        join(d, o)
-
     dqs[...] = (dqt[...] * scale).T.astype(BF16).reshape(2, rows, hd)
     x_dq = remote(dqs.at[g], gq_ref.at[h], x_s.at[3], x_r.at[3], partner)
     x_dq_in = remote(dqs.at[g], gq_ref.at[g], x_s.at[3], x_r.at[3], partner)
     x_dq.start()
     gq_ref[h] = dqs[h]
+
+    for d, o in ROOTS:
+        join(d, o)
 
     def pf_out(i):
         return remote(pf, pf, pf_s.at[i], pf_r.at[0], {"resp": (r + i) % nr})

time: 70.9 us -> 70.7 us (level)
  the two profiles are of different devices: /device:TPU:27 before, /device:TPU:14 now
where the time goes in v4:
time: 70.7 us; the launch traced here: 70.5 us
  Pallas kernels  69.9 us (99%)
    pallas_call x1, Pallas kernels, per_device(): pl.pallas_call(functools.partial(kernel, nz=nz, nr=nr, tok=tok, heads=hea...  68.1 us
    pallas_call x1, Pallas kernels, per_device(): pl.pallas_call(write_out, name='write_out', out_shape=tuple((jax.ShapeDty...  1.75 us

profile of v4, /device:TPU:14, one launch (start us, length us, event | category | flops | bytes accessed | tf_op | source)
XLA Modules:
  0.0 70.5 jit_solution(10861544694222862237)
XLA Ops:
  0.6 68.1 %grpo_backward.1 = (bf16[2,512,128]{2,1,0:T(8,128)(2,1)}, bf16[2,64,128]{2,1,0:T(8,128)(2,1)}, bf16[2,64,128]{2,1,0:T(8,128)(2,1)}, f32[16,128]{1,0:T(8,128)}, f32[16,128]{1,0:T(8,128)}) custom-call(bf16[2,512,128]{2,1,0:T(8,128)(2,1)} %bitcast.3, bf16[2,512,128]{2,1,0:T(8,128)(2,1)} %bitcast.4, bf16[16,128]{1,0:T(8,128)(2,1)} %pk_ref.1, ...), custom_call_target="tpu_custom_call" | custom-call | tf_op jit(solution)/shard_map/grpo_backward/pallas_call | solution.py:598
  68.8 1.8 %write_out.1 = (bf16[2,64,8,128]{3,2,1,0:T(8,128)(2,1)}, bf16[2,64,128]{2,1,0:T(8,128)(2,1)}, bf16[2,64,128]{2,1,0:T(8,128)(2,1)}, f32[16,128]{1,0:T(8,128)}, f32[16,128]{1,0:T(8,128)}) custom-call(bf16[2,64,8,128]{3,2,1,0:T(8,128)(2,1)} %bitcast.5, bf16[2,64,128]{2,1,0:T(8,128)(2,1)} %get-tuple-element.11.refs_1_, ...), custom_call_target="tpu_custom_call" | custom-call | tf_op jit(solution)/shard_map/write_out/pallas_call | solution.py:661
